TPU v7x, 32 devices: a whole 2x2x4 slice. The times are simulated.
32 devices in a mesh: parts: 2 (over y), ctx: 4 (over z), head: 4 (over x, core).
Axes of the slice: x: 2, y: 2, z: 4, core: 2. Of those that a mesh axis runs over, the one named last changes fastest.
Arguments:
- event_ids: int32 [8192], P(('parts', 'ctx')), parts along dimension 0, may hold values from 0 to 255
- embed_table: bfloat16 [256, 1024], replicated, may hold values from -6 to 6
- w_qkv: bfloat16 [1024, 3072], P(None, 'head'), may hold values from -0.1875 to 0.1875
- norm_gain: float32 [1024], P('head'), may hold values from 0.1 to 1.9
- w_out: bfloat16 [1024, 1024], P('head'), may hold values from -0.1875 to 0.1875
- init_state: float32 [8, 128, 128], P('head'), may hold values from -6 to 6
- out_grad: bfloat16 [8192, 1024], P(('parts', 'ctx')), parts along dimension 0, may hold values from -1 to 1
Outputs:
- layer_out: bfloat16 [8192, 1024], P(('parts', 'ctx'), 'head'), parts along dimension 0
- grad_wqkv: float32 [2048, 3072], P(('parts', 'ctx'), 'head'), parts along dimension 0
- grad_wout: float32 [2048, 1024], P(('parts', 'head'), 'ctx'), parts along dimension 0
- grad_gain: float32 [2048], P(('parts', 'head')), parts along dimension 0
- grad_init: float32 [16, 128, 128], P(('parts', 'head')), parts along dimension 0
- grad_table: float32 [512, 1024], P('parts'), parts along dimension 0
There are 2 independent parts, one for each index of `parts`. A program takes and returns all parts, laid end to end along the dimension named above; an argument that names none is the same for every part. Nothing has to cross between parts.
All inputs are finite; a program needn't handle non-finite values.
Results may differ from a plain program's by a relative error of at most 0.0082.
Values sent between devices are 32-bit elements; how exact they have to be, the bound alone decides.
A program may use at most 64 MiB of HBM per device.

v0:
```python
import jax
import jax.numpy as jnp
from jax import lax
from jax.sharding import PartitionSpec as P

BLOCK = 128
EPS = 1e-05


def prefix(part, axis, combine, identity, reverse):
    count = lax.axis_size(axis)
    place = lax.axis_index(axis)
    ahead = count - 1 - place if reverse else place
    gathered = lax.all_gather(part, axis)
    state = jnp.zeros_like(part) + jnp.asarray(identity, part.dtype)

    def one(step, state):
        source = count - 1 - step if reverse else step
        return combine(state, lax.dynamic_index_in_dim(gathered, source, 0, False))

    return lax.fori_loop(0, ahead, one, state)


def lower_mask(block_len):
    rows_idx = lax.broadcasted_iota(jnp.int32, (block_len, block_len), 0)
    cols_idx = lax.broadcasted_iota(jnp.int32, (block_len, block_len), 1)
    return rows_idx >= cols_idx


def add_states(earlier, later_one):
    return earlier + later_one


def contract_rows(left, right):
    return lax.dot_general(
        left, right, (((0,), (0,)), ((), ())), preferred_element_type=jnp.float32
    )


def contract_cols(left, right):
    return lax.dot_general(
        left, right, (((1,), (1,)), ((), ())), preferred_element_type=jnp.float32
    )


def per_device(event_ids, embed_table, w_qkv, norm_gain, w_out, init_state, out_grad):
    highest = lax.Precision.HIGHEST
    tok_rows = event_ids.shape[0]
    vocab_size = embed_table.shape[0]
    head_local = init_state.shape[0]
    head_dim = init_state.shape[1]
    block_len = BLOCK
    blocks = tok_rows // block_len
    one_hot = event_ids[:, None] == lax.broadcasted_iota(jnp.int32, (1, vocab_size), 1)
    embedded = jnp.dot(
        one_hot.astype(jnp.bfloat16), embed_table, preferred_element_type=jnp.float32
    ).astype(jnp.bfloat16)
    projected = jnp.dot(embedded, w_qkv, preferred_element_type=jnp.float32).astype(jnp.bfloat16)
    shaped = projected.reshape(blocks, block_len, head_local, 3, head_dim)
    queries = shaped[:, :, :, 0]
    key_rows = shaped[:, :, :, 1]
    value_rows = shaped[:, :, :, 2]
    block_kv = jnp.einsum(
        "bshd,bshe->bhde", key_rows, value_rows, preferred_element_type=jnp.float32
    )
    own_total = jnp.sum(block_kv, axis=0)
    zero_state = jnp.zeros_like(own_total)
    earlier_state = prefix(own_total, "ctx", add_states, zero_state, False)
    cumulative = jnp.cumsum(block_kv, axis=0)
    shifted = jnp.concatenate([jnp.zeros_like(block_kv[:1]), cumulative[:-1]], axis=0)
    states = init_state[None] + earlier_state[None] + shifted
    mask_tri = lower_mask(block_len)[None, None]
    scores = jnp.einsum("bthd,bshd->bhts", queries, key_rows, preferred_element_type=jnp.float32)
    scores_bf = jnp.where(mask_tri, scores, 0.0).astype(jnp.bfloat16)
    inter = jnp.einsum("bthd,bhde->bthe", queries.astype(jnp.float32), states, precision=highest)
    intra = jnp.einsum("bhts,bshe->bthe", scores_bf, value_rows, preferred_element_type=jnp.float32)
    raw_out = inter + intra
    inv_rms = lax.rsqrt(jnp.mean(raw_out * raw_out, axis=-1, keepdims=True) + EPS)
    normed = raw_out * inv_rms
    gain_view = norm_gain.reshape(head_local, head_dim)
    attn = (normed * gain_view).astype(jnp.bfloat16).reshape(tok_rows, head_local * head_dim)
    head_terms = jnp.dot(attn, w_out, preferred_element_type=jnp.float32)
    mixed = lax.psum_scatter(head_terms, "head", scatter_dimension=1, tiled=True)
    out_cols = mixed.shape[1]
    residual = lax.dynamic_slice_in_dim(embedded, lax.axis_index("head") * out_cols, out_cols, 1)
    layer_out = (residual.astype(jnp.float32) + mixed).astype(jnp.bfloat16)
    grad_attn = contract_cols(out_grad, w_out)
    grad_wout_local = contract_rows(attn, out_grad)
    normed_flat = normed.reshape(tok_rows, head_local * head_dim)
    grad_gain_local = jnp.sum(grad_attn * normed_flat, axis=0)
    grad_norm = (grad_attn * norm_gain).reshape(blocks, block_len, head_local, head_dim)
    grad_raw = inv_rms * (grad_norm - normed * jnp.mean(grad_norm * normed, axis=-1, keepdims=True))
    grad_bf = grad_raw.astype(jnp.bfloat16)
    grad_scores = jnp.einsum(
        "bthe,bshe->bhts", grad_bf, value_rows, preferred_element_type=jnp.float32
    )
    grad_scores = jnp.where(mask_tri, grad_scores, 0.0).astype(jnp.bfloat16)
    block_qg = jnp.einsum("bthd,bthe->bhde", queries, grad_bf, preferred_element_type=jnp.float32)
    own_grad = jnp.sum(block_qg, axis=0)
    later_state = prefix(own_grad, "ctx", add_states, zero_state, True)
    reversed_sum = jnp.cumsum(block_qg[::-1], axis=0)[::-1]
    local_after = jnp.concatenate([reversed_sum[1:], jnp.zeros_like(block_qg[:1])], axis=0)
    after = later_state[None] + local_after
    grad_q = jnp.einsum(
        "bthe,bhde->bthd", grad_bf.astype(jnp.float32), states, precision=highest
    ) + jnp.einsum("bhts,bshd->bthd", grad_scores, key_rows, preferred_element_type=jnp.float32)
    grad_k = jnp.einsum(
        "bshe,bhde->bshd", value_rows.astype(jnp.float32), after, precision=highest
    ) + jnp.einsum("bhts,bthd->bshd", grad_scores, queries, preferred_element_type=jnp.float32)
    grad_v = jnp.einsum(
        "bshd,bhde->bshe", key_rows.astype(jnp.float32), after, precision=highest
    ) + jnp.einsum("bhts,bthe->bshe", scores_bf, grad_bf, preferred_element_type=jnp.float32)
    grad_proj = (
        jnp.stack([grad_q, grad_k, grad_v], axis=3)
        .astype(jnp.bfloat16)
        .reshape(tok_rows, head_local * 3 * head_dim)
    )
    vocab_proj = contract_rows(one_hot.astype(jnp.bfloat16), grad_proj)
    vocab_cot = contract_rows(one_hot.astype(jnp.bfloat16), out_grad)
    summed_vocab, summed_wout, summed_gain, grad_init, summed_cot = lax.psum(
        (vocab_proj, grad_wout_local, grad_gain_local, own_grad, vocab_cot), "ctx"
    )
    summed_wqkv = lax.dot_general(
        embed_table.astype(jnp.float32),
        summed_vocab,
        (((0,), (0,)), ((), ())),
        precision=highest,
        preferred_element_type=jnp.float32,
    )
    head_table = lax.dot_general(
        summed_vocab,
        w_qkv.astype(jnp.float32),
        (((1,), (1,)), ((), ())),
        precision=highest,
        preferred_element_type=jnp.float32,
    )
    grad_table = lax.psum(head_table, "head") + summed_cot
    ctx_pos = lax.axis_index("ctx")
    width_rows = summed_wqkv.shape[0] // lax.axis_size("ctx")
    own_wqkv = lax.dynamic_slice_in_dim(summed_wqkv, ctx_pos * width_rows, width_rows, 0)
    own_wout = lax.dynamic_slice_in_dim(summed_wout, ctx_pos * width_rows, width_rows, 1)
    return (layer_out, own_wqkv, own_wout, summed_gain, grad_init, grad_table)


def solution(mesh):
    in_specs = (
        P(("parts", "ctx")),
        P(),
        P(None, "head"),
        P("head"),
        P("head", None),
        P("head", None, None),
        P(("parts", "ctx"), None),
    )
    out_specs = (
        P(("parts", "ctx"), "head"),
        P(("parts", "ctx"), "head"),
        P(("parts", "head"), "ctx"),
        P(("parts", "head")),
        P(("parts", "head"), None, None),
        P("parts", None),
    )
    return jax.shard_map(
        per_device, mesh=mesh, in_specs=in_specs, out_specs=out_specs, check_vma=False
    )
```

profile of v0, /device:TPU:0, one launch (start us, length us, event | category | flops | bytes accessed | tf_op | source)
XLA Modules:
  0.0 317.2 jit_solution(2077347792032638478)
XLA Ops:
  7.3 1.5 copy-done
  8.8 2.7 fusion.13
  11.4 0.8 convolution_convert_fusion
  12.2 1.3 copy-done.14
  13.6 3.0 convolution_convert_fusion.1
  16.5 2.6 copy.49
  19.1 1.8 copy.89
  21.0 1.1 fusion.47
  22.0 0.4 copy.88
  22.4 1.6 copy.87
  24.0 2.3 fusion.48
  26.3 18.0 %all-gather = f32[8,128,128]{2,1,0:T(8,128)} all-gather(f32[2,128,128]{2,1,0:T(8,128)S(1)} %get-tuple-element.134), channel_id=2, replica_groups=mesh['parts'=2,'ctx'=4,'head'=4] {'ctx'}, dimensions={0}, use_global_device_ids=true | all-gather | bytes 655360 | tf_op jit(solution)/shard_map/all_gather | solution.py:14
  44.4 1.4 fusion.50
  45.7 0.1 slice.26
  45.8 0.3 fusion.4
  46.1 0.5 copy-done.25
  46.6 1.0 fusion.16
  47.7 1.5 multiply_reduce_fusion.1
  49.2 2.1 broadcast_multiply_fusion
  51.3 2.7 reshape.58
  54.0 2.2 copy.59
  56.3 1.8 multiply_reduce_fusion
  58.1 1.1 multiply_convert_fusion
  59.2 0.6 copy-done.11
  59.8 1.6 fusion.15
  61.5 1.3 fusion.5
  62.8 1.5 fusion.49
  64.3 2.4 rev.4
  66.7 1.3 fusion.51
  68.0 1.0 slice.28
  69.0 2.2 slice.23
  71.2 19.9 %all-gather.1 = f32[8,128,128]{2,1,0:T(8,128)} all-gather(f32[2,128,128]{2,1,0:T(8,128)S(1)} %get-tuple-element.138), channel_id=3, replica_groups=mesh['parts'=2,'ctx'=4,'head'=4] {'ctx'}, dimensions={0}, use_global_device_ids=true | all-gather | bytes 655360 | tf_op jit(solution)/shard_map/all_gather | solution.py:14
  91.2 3.1 while.23
  91.2 0.9 bitcast_add_fusion.5
  92.1 0.9 bitcast_add_fusion.5
  93.1 0.9 bitcast_add_fusion.5
  94.3 2.5 fusion.18
  96.8 1.0 fusion.17
  97.8 0.3 copy.56
  98.2 1.7 fusion.20
  99.9 0.5 fusion.11
  100.4 0.5 copy-done.6
  100.9 0.4 fusion.10
  101.3 0.3 fusion.9
  101.6 0.2 pad_maximum_fusion
  101.8 1.0 copy.67
  102.8 1.7 fusion
  104.5 0.0 all-reduce.6.cloned.1.call-start
  104.6 116.2 %all-reduce.8.cloned.1.call-done = (f32[256,768]{1,0:T(8,128)}, f32[256,1024]{1,0:T(8,128)}, f32[2,128,128]{2,1,0:T(8,128)}, f32[256,1024]{1,0:T(8,128)}) async-done(((f32[256,768]{1,0:T(8,128)}, f32[256,1024]{1,0:T(8,128)}, f32[2,128,128]{2,1,0:T(8,128)}, f32[256,1024]{1,0:T(8,128)}), (f32[256,768]{1,0:T(8,128)}, f32[256,1024]{1,0:T(8,128)}, f32[2,128,128]{2,1,0:T(8,128)}, ...) | async-done | bytes 3014672 | tf_op jit(solution)/shard_map/psum | solution.py:120
  220.8 4.2 %fusion.53 = f32[256,1024]{1,0:T(8,128)} fusion(f32[256,768]{1,0:T(8,128)} %get-tuple-element.121, bf16[1024,768]{1,0:T(8,128)(2,1)} %param.13), kind=kOutput, calls=%fused_computation.80 | convolution fusion | flops 2415919104 | bytes 3407872 | tf_op jit(solution)/shard_map/dot_general | solution.py:130
  225.0 2.7 fusion.22
  227.8 1.2 copy-done.2
  229.0 1.3 copy.84
  230.3 1.8 fusion.12
  232.1 10.0 %psum.44 = f32[256]{0:T(256)} all-reduce(f32[256]{0:T(256)S(1)} %fusion.12), channel_id=1, replica_groups=mesh['parts'=2,'ctx'=4,'head'=4] {'ctx'}, use_global_device_ids=true, to_apply=%region_14.15 | all-reduce | flops 256 | bytes 2048 | tf_op jit(solution)/shard_map/psum | solution.py:120
  242.1 1.4 fusion.52
  243.5 0.1 dynamic-slice_bitcast_fusion
  243.6 1.1 copy.70
  244.8 1.7 constant_dynamic-slice_fusion
  246.4 13.7 %all-reduce.6.cloned.1.call-done = f32[256,1024]{1,0:T(8,128)} async-done(((f32[256,1024]{1,0:T(8,128)}), f32[256,1024]{1,0:T(8,128)}) %all-reduce.6.cloned.1.call-update) | async-done | bytes 1048592 | tf_op jit(solution)/shard_map/psum | solution.py:137
  260.1 2.7 add.133
  262.8 44.9 %reduce-scatter.2.cloned.1.call-done = f32[1024,256]{1,0:T(8,128)} async-done(((f32[1024,1024]{1,0:T(8,128)}), f32[1024,256]{1,0:T(8,128)}) %reduce-scatter.2.cloned.1.call-update) | async-done | bytes 1048592 | tf_op jit(solution)/shard_map/reduce_scatter | solution.py:83
  307.7 2.3 add_convert_fusion
  310.0 0.7 copy.130
  (64 shorter events, 0.3 us)
Async XLA Ops:
  7.2 1.6 copy-start
  7.2 4.2 %copy-start.28 = (s32[1024]{0:T(1024)S(1)}, s32[1024]{0:T(1024)}, u32[]{:S(2)}) copy-start(s32[1024]{0:T(1024)} %param.11) | copy-start | bytes 12292
  7.2 4.2 %copy-start.18 = (bf16[256,1024]{1,0:T(8,128)(2,1)S(1)}, bf16[256,1024]{1,0:T(8,128)(2,1)}, u32[]{:S(2)}) copy-start(bf16[256,1024]{1,0:T(8,128)(2,1)} %param.12) | copy-start | bytes 1572868
  7.2 213.6 %all-reduce.8.cloned.1.call-start = ((), (), s32[]{:S(2)}) async-start(), calls=%async_computation.3 | async-start | bytes 6029312 | tf_op jit(solution)/shard_map/psum | solution.py:120
  11.4 2.1 copy-start.23
  12.2 1.4 copy-start.14
  22.4 24.2 %copy-start.4 = (bf16[8,128,2,1,128]{4,1,2,0,3:T(8,128)(2,1)}, bf16[8,128,2,1,128]{4,1,2,0,3:T(8,128)(2,1)S(1)}, u32[]{:S(2)}) copy-start(bf16[8,128,2,1,128]{4,1,2,0,3:T(8,128)(2,1)S(1)} %copy.88) | copy-start | bytes 1572868
  44.3 1.5 copy-start.7
  45.7 0.9 copy-start.25
  45.8 1.9 copy-start.10
  46.1 3.1 copy-start.20
  47.7 1.5 copy-start.16
  47.7 1.5 copy-start.27
  56.3 1.9 copy-start.3
  58.1 3.4 %copy-start.1 = (f32[8,128,2,128]{1,3,2,0:T(8,128)}, f32[8,128,2,128]{1,3,2,0:T(8,128)S(1)}, u32[]{:S(2)}) copy-start(f32[8,128,2,128]{1,3,2,0:T(8,128)S(1)} %get-tuple-element.126) | copy-start | bytes 3145732
  58.1 1.8 copy-start.11
  59.8 3.0 copy-start.5
  64.3 6.9 %copy-start.24 = (f32[2,128,128]{2,1,0:T(8,128)}, f32[2,128,128]{2,1,0:T(8,128)S(1)}, u32[]{:S(2)}) copy-start(f32[2,128,128]{2,1,0:T(8,128)S(1)} %get-tuple-element.138) | copy-start | bytes 393220
  94.2 2.6 copy-start.8
  94.2 2.6 copy-start.9
  94.2 3.6 %copy-start.22 = (bf16[8,128,2,128]{1,3,2,0:T(8,128)(2,1)S(1)}, bf16[8,128,2,128]{1,3,2,0:T(8,128)(2,1)}, u32[]{:S(2)}) copy-start(bf16[8,128,2,128]{1,3,2,0:T(8,128)(2,1)} %get-tuple-element.131) | copy-start | bytes 1572868
  98.2 1.7 copy-start.12
  98.2 1.7 copy-start.13
  99.9 1.0 copy-start.6
  99.9 1.4 copy-start.21
  104.5 155.6 %all-reduce.6.cloned.1.call-start = ((), (), s32[]{:S(2)}) async-start(), calls=%async_computation.2 | async-start | bytes 2097152 | tf_op jit(solution)/shard_map/psum | solution.py:137
  220.8 4.2 %copy-start.17 = (bf16[256,1024]{1,0:T(8,128)(2,1)S(1)}, bf16[256,1024]{1,0:T(8,128)(2,1)}, u32[]{:S(2)}) copy-start(bf16[256,1024]{1,0:T(8,128)(2,1)} %param.15) | copy-start | bytes 1572868
  225.0 82.8 %reduce-scatter.2.cloned.1.call-start = ((), (), s32[]{:S(2)}) async-start(), calls=%async_computation.1 | async-start | bytes 5242880 | tf_op jit(solution)/shard_map/reduce_scatter | solution.py:83
  227.7 1.2 copy-start.2
  230.2 11.8 %copy-start.15 = (f32[256,768]{1,0:T(8,128)S(1)}, f32[256,768]{1,0:T(8,128)}, u32[]{:S(2)}) copy-start(f32[256,768]{1,0:T(8,128)} %get-tuple-element.121) | copy-start | bytes 2359300
  230.3 11.8 %copy-start.19 = (bf16[256,1024]{1,0:T(8,128)(2,1)S(1)}, bf16[256,1024]{1,0:T(8,128)(2,1)}, u32[]{:S(2)}) copy-start(bf16[256,1024]{1,0:T(8,128)(2,1)} %param.12) | copy-start | bytes 1572868
  260.1 49.9 %copy-start.26 = (f32[2,128,128]{2,1,0:T(8,128)S(1)}, f32[2,128,128]{2,1,0:T(8,128)}, u32[]{:S(2)}) copy-start(f32[2,128,128]{2,1,0:T(8,128)} %get-tuple-element.241) | copy-start | bytes 393220
Sparse Core Ops, SparseCore 0:
  104.6 116.0 all-reduce.7
  225.1 34.9 all-reduce.5
  262.8 44.8 reduce-scatter.1
where the time goes:
time: 318 us; the launch traced here: 317 us
  waiting for transfers between devices  175 us (55%)
  blocking collectives  47.9 us (15%)
  matrix products  34.4 us (11%)
  local copies, waits for them, and re-layouts  30.1 us (9%)
  other arithmetic  15.4 us (5%)
  between operations  14.2 us (4%)
    psum x1, waiting for transfers between devices, per_device(): lax.psum((vocab_proj, grad_wout_local, grad_gain_local, own_grad, vocab_c...  116 us
    reduce_scatter x1, waiting for transfers between devices, per_device(): lax.psum_scatter(head_terms, 'head', scatter_dimension=1, tiled=True)  44.9 us
    all_gather x2, blocking collectives, prefix(): gathered = lax.all_gather(part, axis)  37.9 us
    psum x1, waiting for transfers between devices, per_device(): grad_table = lax.psum(head_table, 'head') + summed_cot  13.7 us
    unnamed x63, local copies, waits for them, and re-layouts  11.4 us
    psum x1, blocking collectives, per_device(): lax.psum((vocab_proj, grad_wout_local, grad_gain_local, own_grad, vocab_c...  10 us
  transfers between devices with their start and end apart: 3, of which 3 were waited for; matrix products, arithmetic and copies ran while one was open for 4% of the time, Pallas kernels for 0%

commit v1 on v0

--- a/solution.py
+++ b/solution.py
@@ -134,7 +134,7 @@
         precision=highest,
         preferred_element_type=jnp.float32,
     )
-    grad_table = lax.psum(head_table, "head") + summed_cot
+    grad_table = jnp.sum(lax.all_gather(head_table, "head"), axis=0) + summed_cot
     ctx_pos = lax.axis_index("ctx")
     width_rows = summed_wqkv.shape[0] // lax.axis_size("ctx")
     own_wqkv = lax.dynamic_slice_in_dim(summed_wqkv, ctx_pos * width_rows, width_rows, 0)

time: 318 us -> 273 us (0.86)
  waiting for transfers between devices: 175 us -> 126 us
    reduce_scatter x1, waiting for transfers between devices: 44.9 us -> 0.01 us  [per_device(): lax.psum_scatter(head_terms, 'head', scatter_dimension=1, tiled=True)]
    psum x1 -> x0, waiting for transfers between devices: 13.7 us -> none  [per_device(): grad_table = lax.psum(head_table, 'head') + summed_cot]
    all_gather x0 -> x1, waiting for transfers between devices: none -> 13.6 us  [per_device(): lax.all_gather(head_table, 'head')]
    psum x1, waiting for transfers between devices: 116 us -> 112 us  [per_device(): lax.psum((vocab_proj, grad_wout_local, grad_gain_local, own_grad, vocab_c...]
  transfers between devices with their start and end apart: 3 -> 3, of which waited for: 3 -> 2; matrix products, arithmetic and copies ran while one was open for 4% -> 6% of each run, Pallas kernels for 0% -> 0%
where the time goes in v1:
time: 273 us; the launch traced here: 272 us
  waiting for transfers between devices  126 us (46%)
  blocking collectives  47.9 us (18%)
  matrix products  34.4 us (13%)
  local copies, waits for them, and re-layouts  29.9 us (11%)
  other arithmetic  17.8 us (7%)
  between operations  15.9 us (6%)
    psum x1, waiting for transfers between devices, per_device(): lax.psum((vocab_proj, grad_wout_local, grad_gain_local, own_grad, vocab_c...  112 us
    all_gather x2, blocking collectives, prefix(): gathered = lax.all_gather(part, axis)  37.9 us
    all_gather x1, waiting for transfers between devices, per_device(): lax.all_gather(head_table, 'head')  13.6 us
    unnamed x63, local copies, waits for them, and re-layouts  11.2 us
    psum x1, blocking collectives, per_device(): lax.psum((vocab_proj, grad_wout_local, grad_gain_local, own_grad, vocab_c...  10 us
    dot_general x3, matrix products, contract_rows(): lax.dot_general(left, right, (((0,), (0,)), ((), ())), preferred_element_...  6.04 us
  transfers between devices with their start and end apart: 3, of which 2 were waited for; matrix products, arithmetic and copies ran while one was open for 6% of the time, Pallas kernels for 0%

profile of v1, /device:TPU:0, one launch (start us, length us, event | category | flops | bytes accessed | tf_op | source)
XLA Modules:
  0.0 272.3 jit_solution(18029594449375735400)
XLA Ops:
  8.1 1.5 copy-done
  9.6 2.7 fusion.13
  12.3 0.8 convolution_convert_fusion
  13.0 1.4 copy-done.14
  14.4 3.0 %convolution_convert_fusion.1 = bf16[1024,768]{1,0:T(8,128)(2,1)} fusion(bf16[1024,1024]{1,0:T(8,128)(2,1)S(1)} %convolution_convert_fusion, bf16[1024,768]{1,0:T(8,128)(2,1)S(1)} %copy-done.23), kind=kOutput, calls=%fused_computation.3 | convolution fusion | flops 1611399168 | bytes 5242880 | tf_op jit(solution)/shard_map/dot_general | solution.py:58
  17.4 2.6 copy.49
  20.0 1.8 copy.89
  21.8 1.1 fusion.47
  22.9 0.4 copy.88
  23.3 1.6 copy.87
  24.9 2.3 fusion.48
  27.2 18.0 %all-gather = f32[8,128,128]{2,1,0:T(8,128)} all-gather(f32[2,128,128]{2,1,0:T(8,128)S(1)} %get-tuple-element.134), channel_id=2, replica_groups=mesh['parts'=2,'ctx'=4,'head'=4] {'ctx'}, dimensions={0}, use_global_device_ids=true | all-gather | bytes 655360 | tf_op jit(solution)/shard_map/all_gather | solution.py:14
  45.2 1.4 fusion.50
  46.6 0.1 slice.26
  46.7 0.3 fusion.4
  47.0 0.5 copy-done.25
  47.5 1.0 fusion.16
  48.5 1.5 multiply_reduce_fusion.1
  50.1 2.1 broadcast_multiply_fusion
  52.1 2.7 %reshape.59 = f32[8,128,2,128]{3,2,1,0:T(2,128)} reshape(f32[1024,256]{1,0:T(8,128)} %get-tuple-element.132) | data formatting | bytes 2097152 | tf_op jit(solution)/shard_map/reshape | solution.py:91
  54.9 2.2 copy.59
  57.1 1.8 multiply_reduce_fusion
  59.0 1.1 multiply_convert_fusion
  60.1 0.6 copy-done.11
  60.7 1.6 fusion.15
  62.3 1.3 fusion.5
  63.7 1.5 fusion.49
  65.2 2.4 rev.4
  67.5 1.3 fusion.51
  68.8 1.0 slice.28
  69.8 2.2 slice.23
  72.1 19.9 %all-gather.1 = f32[8,128,128]{2,1,0:T(8,128)} all-gather(f32[2,128,128]{2,1,0:T(8,128)S(1)} %get-tuple-element.138), channel_id=3, replica_groups=mesh['parts'=2,'ctx'=4,'head'=4] {'ctx'}, dimensions={0}, use_global_device_ids=true | all-gather | bytes 655360 | tf_op jit(solution)/shard_map/all_gather | solution.py:14
  92.0 3.1 %while.23 = (s32[]{:T(128)}, f32[2,128,128]{2,1,0:T(8,128)S(1)}, s32[]{:T(128)}, f32[4,2,128,128]{3,2,1,0:T(8,128)}, s32[]{:T(128)}, /*index=5*/s32[]{:T(128)}, s32[]{:T(128)}, s32[]{:T(128)}) while((s32[]{:T(128)}, f32[2,128,128]{2,1,0:T(8,128)S(1)}, s32[]{:T(128)}, f32[4,2,128,128]{3,2,1,0:T(8,128)}, s32[]{:T(128)}, /*index=5*/s32[]{:T(128)}, ...), condition=%wide.region_9.10_spmd, body=%wide.region_8.9_spmd.sunk | while | flops 32774 | bytes 393359 | solution.py:21
  92.0 0.9 bitcast_add_fusion.5
  93.0 0.9 bitcast_add_fusion.5
  93.9 0.9 bitcast_add_fusion.5
  95.1 2.5 fusion.18
  97.6 1.0 fusion.17
  98.7 0.3 copy.56
  99.0 1.7 fusion.20
  100.7 0.5 fusion.11
  101.2 0.5 copy-done.6
  101.8 0.4 fusion.10
  102.1 0.3 fusion.9
  102.4 0.2 pad_maximum_fusion
  102.6 1.0 copy.67
  103.6 1.7 fusion
  105.4 1.0 copy-done.17
  106.4 2.7 %fusion.22 = f32[1024,1024]{1,0:T(8,128)} fusion(bf16[256,1024]{1,0:T(8,128)(2,1)S(1)} %copy-done.17, bf16[32,8,8,128]{3,2,1,0:T(8,128)(2,1)S(1)} %bitcast.110), kind=kOutput, calls=%fused_computation.42 | convolution fusion | flops 536870912 | bytes 5242880 | tf_op jit(solution)/shard_map/dot_general | solution.py:82
  109.1 0.0 all-gather.5.cloned.1.call-start
  109.2 112.4 %all-reduce.5.cloned.1.call-done = (f32[256,768]{1,0:T(8,128)}, f32[256,1024]{1,0:T(8,128)}, f32[2,128,128]{2,1,0:T(8,128)}, f32[256,1024]{1,0:T(8,128)}) async-done(((f32[256,768]{1,0:T(8,128)}, f32[256,1024]{1,0:T(8,128)}, f32[2,128,128]{2,1,0:T(8,128)}, f32[256,1024]{1,0:T(8,128)}), (f32[256,768]{1,0:T(8,128)}, f32[256,1024]{1,0:T(8,128)}, f32[2,128,128]{2,1,0:T(8,128)}, ...) | async-done | bytes 3014672 | tf_op jit(solution)/shard_map/psum | solution.py:120
  221.6 4.2 %fusion.53 = f32[256,1024]{1,0:T(8,128)} fusion(f32[256,768]{1,0:T(8,128)} %get-tuple-element.121, bf16[1024,768]{1,0:T(8,128)(2,1)} %param.13), kind=kOutput, calls=%fused_computation.80 | convolution fusion | flops 2415919104 | bytes 3407872 | tf_op jit(solution)/shard_map/dot_general | solution.py:130
  225.8 1.3 copy.84
  227.1 1.8 fusion.12
  228.9 10.0 %psum.37 = f32[256]{0:T(256)} all-reduce(f32[256]{0:T(256)S(1)} %fusion.12), channel_id=1, replica_groups=mesh['parts'=2,'ctx'=4,'head'=4] {'ctx'}, use_global_device_ids=true, to_apply=%region_14.15 | all-reduce | flops 256 | bytes 2048 | tf_op jit(solution)/shard_map/psum | solution.py:120
  238.9 1.4 fusion.52
  240.4 0.1 dynamic-slice_bitcast_fusion
  240.5 1.1 copy.70
  241.6 1.7 constant_dynamic-slice_fusion
  243.3 2.3 add_convert_fusion
  245.5 13.6 %all-gather.5.cloned.1.call-done = f32[1024,1024]{1,0:T(8,128)} async-done(((f32[256,1024]{1,0:T(8,128)}), f32[1024,1024]{1,0:T(8,128)}) %all-gather.5.cloned.1.call-update) | async-done | bytes 4194320 | tf_op jit(solution)/shard_map/all_gather | solution.py:137
  259.1 2.7 reduce_sum.59
  261.8 2.4 add.131
  264.2 0.7 copy.130
  (65 shorter events, 0.4 us)
Async XLA Ops:
  8.0 1.6 copy-start
  8.0 4.2 %copy-start.28 = (s32[1024]{0:T(1024)S(1)}, s32[1024]{0:T(1024)}, u32[]{:S(2)}) copy-start(s32[1024]{0:T(1024)} %param.11) | copy-start | bytes 12292
  8.0 4.2 %copy-start.18 = (bf16[256,1024]{1,0:T(8,128)(2,1)S(1)}, bf16[256,1024]{1,0:T(8,128)(2,1)}, u32[]{:S(2)}) copy-start(bf16[256,1024]{1,0:T(8,128)(2,1)} %param.12) | copy-start | bytes 1572868
  8.0 213.6 %all-reduce.5.cloned.1.call-start = ((), (), s32[]{:S(2)}) async-start(), calls=%async_computation.3 | async-start | bytes 6029312 | tf_op jit(solution)/shard_map/psum | solution.py:120
  12.3 2.1 copy-start.23
  13.0 1.4 copy-start.14
  23.3 24.2 %copy-start.4 = (bf16[8,128,2,1,128]{4,1,2,0,3:T(8,128)(2,1)}, bf16[8,128,2,1,128]{4,1,2,0,3:T(8,128)(2,1)S(1)}, u32[]{:S(2)}) copy-start(bf16[8,128,2,1,128]{4,1,2,0,3:T(8,128)(2,1)S(1)} %copy.88) | copy-start | bytes 1572868
  45.2 1.5 copy-start.7
  46.6 0.9 copy-start.25
  46.7 1.9 copy-start.10
  47.0 3.1 %copy-start.20 = (bf16[8,2,128,128]{3,2,1,0:T(8,128)(2,1)}, bf16[8,2,128,128]{3,2,1,0:T(8,128)(2,1)S(1)}, u32[]{:S(2)}) copy-start(bf16[8,2,128,128]{3,2,1,0:T(8,128)(2,1)S(1)} %fusion.4) | copy-start | bytes 1572868
  48.5 1.5 copy-start.16
  48.5 1.5 copy-start.27
  57.1 1.9 copy-start.3
  58.9 3.4 %copy-start.1 = (f32[8,128,2,128]{1,3,2,0:T(8,128)}, f32[8,128,2,128]{1,3,2,0:T(8,128)S(1)}, u32[]{:S(2)}) copy-start(f32[8,128,2,128]{1,3,2,0:T(8,128)S(1)} %get-tuple-element.126) | copy-start | bytes 3145732
  58.9 1.8 copy-start.11
  60.7 3.0 %copy-start.5 = (bf16[8,128,2,1,128]{4,1,2,0,3:T(8,128)(2,1)S(1)}, bf16[8,128,2,1,128]{4,1,2,0,3:T(8,128)(2,1)}, u32[]{:S(2)}) copy-start(bf16[8,128,2,1,128]{4,1,2,0,3:T(8,128)(2,1)} %copy-done.4) | copy-start | bytes 1572868
  65.2 6.9 %copy-start.24 = (f32[2,128,128]{2,1,0:T(8,128)}, f32[2,128,128]{2,1,0:T(8,128)S(1)}, u32[]{:S(2)}) copy-start(f32[2,128,128]{2,1,0:T(8,128)S(1)} %get-tuple-element.138) | copy-start | bytes 393220
  95.1 2.6 copy-start.8
  95.1 2.6 copy-start.9
  95.1 3.6 %copy-start.22 = (bf16[8,128,2,128]{1,3,2,0:T(8,128)(2,1)S(1)}, bf16[8,128,2,128]{1,3,2,0:T(8,128)(2,1)}, u32[]{:S(2)}) copy-start(bf16[8,128,2,128]{1,3,2,0:T(8,128)(2,1)} %get-tuple-element.131) | copy-start | bytes 1572868
  99.0 1.7 copy-start.12
  99.0 1.7 copy-start.13
  100.7 1.0 copy-start.6
  100.7 1.4 copy-start.21
  105.3 1.0 copy-start.17
  105.4 137.9 %reduce-scatter.2.cloned.1.call-start = ((), (), s32[]{:S(2)}) async-start(), calls=%async_computation.1 | async-start | bytes 5242880 | tf_op jit(solution)/shard_map/reduce_scatter | solution.py:83
  109.1 150.0 %all-gather.5.cloned.1.call-start = ((), (), s32[]{:S(2)}) async-start(), calls=%async_computation.2 | async-start | bytes 5242880 | tf_op jit(solution)/shard_map/all_gather | solution.py:137
  221.6 4.2 %copy-start.2 = (f32[8,128,2,128]{1,3,2,0:T(8,128)S(1)}, f32[8,128,2,128]{1,3,2,0:T(8,128)}, u32[]{:S(2)}) copy-start(f32[8,128,2,128]{1,3,2,0:T(8,128)} %copy-done.1) | copy-start | bytes 3145732
  227.1 11.8 %copy-start.15 = (f32[256,768]{1,0:T(8,128)S(1)}, f32[256,768]{1,0:T(8,128)}, u32[]{:S(2)}) copy-start(f32[256,768]{1,0:T(8,128)} %get-tuple-element.121) | copy-start | bytes 2359300
  227.1 11.8 %copy-start.19 = (bf16[256,1024]{1,0:T(8,128)(2,1)S(1)}, bf16[256,1024]{1,0:T(8,128)(2,1)}, u32[]{:S(2)}) copy-start(bf16[256,1024]{1,0:T(8,128)(2,1)} %param.12) | copy-start | bytes 1572868
  261.8 2.4 copy-start.26
Sparse Core Ops, SparseCore 0:
  105.5 116.0 all-reduce.4
Sparse Core Ops, SparseCore 1:
  109.2 42.6 reduce-scatter.1
  225.9 33.2 all-gather.4
